TPU v7x, 32 devices: a whole 2x2x4 slice. The times are simulated.
32 devices in a mesh: dp: 8 (over z, x), mp: 4 (over y, core).
Axes of the slice: x: 2, y: 2, z: 4, core: 2. Of those that a mesh axis runs over, the one named last changes fastest.
Arguments:
- features: bfloat16 [8, 320, 128, 128], P('dp', 'mp'), may hold values from -6 to 6
- w_out: bfloat16 [320, 36], P('mp'), may hold values from -0.109375 to 0.109375
- noisy_latent: float32 [8, 4, 128, 128], P('dp', None, 'mp'), may hold values from -6 to 6
- timestep: int32 [8], P('dp'), may hold values from 100 to 699
- w_in: bfloat16 [9, 512, 4], replicated, may hold values from -1 to 1
- b_in: float32 [512], replicated, may hold values from -3 to 3
- w_mid: bfloat16 [9, 512, 512], replicated, may hold values from -0.09375 to 0.09375
- b_mid: float32 [512], replicated, may hold values from -3 to 3
- reward_head: float32 [512], replicated, may hold values from -6 to 6
Outputs:
- feature_grads: bfloat16 [8, 320, 128, 128], P('dp', 'mp')
- weight_grad: float32 [320, 36], P('mp')
All inputs are finite; a program needn't handle non-finite values.
Results may differ from a plain program's by a relative error of at most 0.012.
Values may be sent and summed in bfloat16 or wider, within the bound.
No kernel may reach another device: no remote copies, remote signals or barrier semaphores. Data moves between devices by JAX's collectives and lax.ppermute only.
A program may use at most 192 MiB of HBM per device.

v0:
```python
import functools

import jax
import jax.numpy as jnp
import numpy as np
from jax import lax
from jax.experimental import pallas as pl
from jax.experimental.pallas import tpu as pltpu
from jax.sharding import PartitionSpec as P

BLOCK = 16
WIDE = 32
HALO = 4
TILE = 4
PT_A = 0.5**0.5
PT_B = 2.0**0.5
STEPS = 1000
CHUNK = 9
LANES = 256
PREP_ROWS = 32
QUOTA = 4.5
F32 = jnp.float32
BF16 = jnp.bfloat16


def dot(lhs, rhs, lhs_dim, rhs_dim):
    return lax.dot_general(
        lhs, rhs, (((lhs_dim,), (rhs_dim,)), ((), ())), preferred_element_type=F32
    )


def schedule_table():
    betas = np.linspace(0.00085**0.5, 0.012**0.5, STEPS, dtype=np.float32) ** 2
    table = np.cumprod(np.float32(1.0) - betas, dtype=np.float32)
    return np.pad(table, (0, 1024 - STEPS)).reshape(8, 128)


def roots(table_ref, step):
    rows = lax.broadcasted_iota(jnp.int32, (8, 128), 0)
    cols = lax.broadcasted_iota(jnp.int32, (8, 128), 1)
    hit = jnp.where(rows * 128 + cols == step, table_ref[...], 0.0)
    level = jnp.sum(jnp.sum(hit, axis=1, keepdims=True), axis=0, keepdims=True)
    return jnp.sqrt(level), jnp.sqrt(1.0 - level)


def band_tables(channels, lat):
    wide = BLOCK + 2
    tall = 3 * wide * lat
    picks = np.zeros((3, tall, 9 * lat), np.float32)
    for tap_row in range(3):
        for tap_col in range(3):
            for row in range(wide):
                for chan in range(lat):
                    spot = (tap_col * wide + row) * lat + chan
                    picks[tap_row, spot, (3 * tap_row + tap_col) * lat + chan] = 1.0
    spread = np.kron(np.eye(channels, dtype=np.float32), np.ones((1, BLOCK), np.float32))
    out_row = np.tile(np.repeat(np.arange(wide, dtype=np.int32), lat), 3)
    in_row = np.tile(np.arange(BLOCK, dtype=np.int32), channels)
    thirds = np.concatenate([spread * (in_row % 3 == third) for third in range(3)])
    collect = np.zeros((3, 9 * lat, tall), np.float32)
    for third in range(3):
        for spot in range(tall):
            tap_row = (third - out_row[spot] + 2) % 3
            collect[third, :, spot] = picks[tap_row, spot]
    return out_row, in_row, thirds, collect


def column_tables(cols):
    tiles = cols // TILE
    place = np.arange(cols)
    source = TILE * (place % tiles) + place // tiles
    gather = np.zeros((3, cols, cols), np.float32)
    scatter = np.zeros((3, cols, cols), np.float32)
    for tap_col in range(3):
        for spot in range(cols):
            taken = source[spot] + tap_col - 1
            if 0 <= taken < cols:
                gather[tap_col, taken, spot] = 1.0
                scatter[tap_col, spot, taken] = 1.0
    return gather, scatter.reshape(3 * cols, cols)


def start_blocks(feat_hbm, feat_ref, sems):
    copies = []
    for block in range(feat_hbm.shape[1] // WIDE):
        span = slice(block * WIDE, (block + 1) * WIDE)
        copies.append(
            pltpu.make_async_copy(
                feat_hbm.at[:, span, :], feat_ref.at[:, span, :], sems.at[block]
            )
        )
        copies[-1].start()
    return copies


def pair_of(feat_ref, block):
    channels, _, cols = feat_ref.shape
    parts = [
        feat_ref[:, low : low + BLOCK, :].reshape(channels * BLOCK, cols)
        for low in range(block * WIDE, (block + 1) * WIDE, BLOCK)
    ]
    return jnp.concatenate(parts, axis=1)


def one_hot(hit):
    return jnp.where(hit, 1.0, 0.0).astype(BF16)


def banded(wout_ref, channels, lat):
    group, deep = (BLOCK + 2) * lat, channels * BLOCK
    tall = 3 * group
    place = lax.broadcasted_iota(jnp.int32, (tall, 1), 0)
    tap_col = (place >= group).astype(jnp.int32) + (place >= 2 * group).astype(jnp.int32)
    place = place - group * tap_col
    out_row = lax.div(place, jnp.full_like(place, lat))
    first = lat * tap_col + (place - lat * out_row)
    spot = lax.broadcasted_iota(jnp.int32, (1, deep), 1)
    chan = lax.div(spot, jnp.full_like(spot, BLOCK))
    gap = (spot - BLOCK * chan) - out_row
    spread = one_hot(lax.broadcasted_iota(jnp.int32, (channels, deep), 0) == chan)
    pick = lax.broadcasted_iota(jnp.int32, (tall, 9 * lat), 1)
    band = jnp.zeros((tall, deep), F32)
    for tap_row in range(3):
        taps = dot(one_hot(pick == first + 3 * lat * tap_row), wout_ref[...], 1, 0).astype(BF16)
        band = jnp.where(gap == tap_row - 2, dot(taps, spread, 1, 0), band)
    return band.astype(BF16)


def eps_kernel(step_ref, me_ref, wout_ref, noisy_ref, table_ref, feat_hbm, *refs, parts, rows, lat):
    outs = refs[:parts]
    band_ref, feat_ref, acc_ref, sum_ref, own_ref, sems = refs[parts:]
    channels, height, cols = feat_ref.shape
    copies = start_blocks(feat_hbm, feat_ref, sems)
    group = (BLOCK + 2) * lat
    band = banded(wout_ref, channels, lat)
    band_ref[...] = band
    acc_ref[...] = jnp.zeros(acc_ref.shape, F32)
    _, root_b = roots(table_ref, step_ref[0])
    edge = HALO * lat
    sum_ref[0:edge, :] = jnp.zeros((edge, cols), F32)
    sum_ref[edge + height * lat :, :] = jnp.zeros((edge, cols), F32)
    for chan in range(lat):
        own_ref[pl.ds(chan, rows, stride=lat), :] = noisy_ref[0, chan]
    for pair, copy in enumerate(copies):
        copy.wait()
        part = dot(band, pair_of(feat_ref, pair), 1, 0)
        for half in range(WIDE // BLOCK):
            low = (pair * WIDE + half * BLOCK) * lat
            span = slice(half * cols, (half + 1) * cols)
            for tap_col in range(3):
                acc_ref[tap_col, low : low + group, :] += part[
                    tap_col * group : (tap_col + 1) * group, span
                ]
    spot = lax.broadcasted_iota(jnp.int32, (height * lat, cols), 1)
    inner = slice(lat, lat + height * lat)
    left = jnp.where(spot == 0, 0.0, pltpu.roll(acc_ref[0, inner, :], 1, 1))
    right = jnp.where(spot == cols - 1, 0.0, pltpu.roll(acc_ref[2, inner, :], cols - 1, 1))
    eps = left + acc_ref[1, inner, :] + right
    sum_ref[edge : edge + height * lat, :] = -root_b * eps
    me = me_ref[0]
    low = pl.multiple_of(me * (rows * lat) + edge, 16)
    sum_ref[pl.ds(low, rows * lat), :] += own_ref[...]
    for part in range(parts):
        low = pl.multiple_of((me ^ part) * (rows * lat), 16)
        outs[part][...] = sum_ref[pl.ds(low, (rows + 2 * HALO) * lat), :].astype(BF16)


def prep_kernel(band_ref, wmid_hbm, planes_ref, wmid_ref, band_back_ref, sems):
    chans = wmid_ref.shape[1]
    copies = []
    for tap in range(9):
        copies.append(pltpu.make_async_copy(wmid_hbm.at[tap], wmid_ref.at[tap], sems.at[tap]))
        copies[-1].start()
    band_back_ref[...] = band_ref[...].T
    for tap_row in range(3):
        for tap in range(3 * tap_row, 3 * tap_row + 3):
            copies[tap].wait()
        for low in range(0, chans, PREP_ROWS):
            span = slice(low, low + PREP_ROWS)
            first = wmid_ref[3 * tap_row, span].astype(F32)
            mid = wmid_ref[3 * tap_row + 1, span].astype(F32)
            last = wmid_ref[3 * tap_row + 2, span].astype(F32)
            even = (-2.0 / 3.0) * first + (-1.0 / 3.0) * last
            odd = (-2.0 / 3.0 * PT_A) * mid
            planes_ref[0, tap_row, span] = (even + odd).astype(BF16)
            planes_ref[1, tap_row, span] = (even - odd).astype(BF16)
            even = (1.0 / 6.0) * first + (1.0 / 3.0) * last
            odd = (1.0 / 6.0 * PT_B) * mid
            planes_ref[2, tap_row, span] = (even + odd).astype(BF16)
            planes_ref[3, tap_row, span] = (even - odd).astype(BF16)


def to_planes(cells):
    tiles, chans = cells[0].shape
    none = jnp.zeros((1, chans), F32)
    d0 = jnp.concatenate([none, cells[3][: tiles - 1]], axis=0)
    d1, d2, d3, d4 = cells
    d5 = jnp.concatenate([cells[0][1:], none], axis=0)
    s1, s3 = PT_A * d1, PT_A * d3
    even_a, odd_a = d4 - 2.0 * d2, s3 - 2.0 * s1
    even_b, odd_b = d4 - 0.5 * d2, 2.0 * s3 - s1
    return (
        (d0 + d4) - 2.5 * d2,
        even_a + odd_a,
        even_a - odd_a,
        even_b + odd_b,
        even_b - odd_b,
        (d1 + d5) - 2.5 * d3,
    )


def from_planes(m0, ap, an, bp, bn, m5):
    sum_a, dif_a, sum_b, dif_b = ap + an, PT_A * (ap - an), bp + bn, PT_B * (bp - bn)
    return (
        m0 + sum_a + sum_b,
        dif_a + dif_b,
        0.5 * sum_a + 2.0 * sum_b,
        0.5 * dif_a + 2.0 * dif_b + m5,
    )


def from_planes_back(m0, ap, an, bp, bn, m5):
    sum_a, dif_a, sum_b, dif_b = ap + an, PT_A * (ap - an), bp + bn, PT_B * (bp - bn)
    return (
        m0 - 2.0 * sum_a - 0.5 * sum_b,
        -(2.0 * dif_a + 0.5 * dif_b),
        -(sum_a + sum_b),
        m5 - (dif_a + dif_b),
    )


def chunks_of(rows):
    return [(low, min(low + CHUNK, rows)) for low in range(0, rows, CHUNK)]


def decoder_kernel(step_ref, me_ref, *refs, parts, rows, lat, cols):
    blocks = refs[:parts]
    (table_ref, gather_ref, scatter_ref, taps_ref, bin_ref, bmid_ref, head_ref,
     wmid_ref, planes_ref, out_ref, lat_ref, slope_ref, high_ref, rest_ref, q_ref, lg_ref,
     tapf_ref, win_ref, *bufs) = refs[parts:]
    tiles = cols // TILE
    chans = wmid_ref.shape[1]
    hidden_rows, mixed_rows, grad_rows = rows + 6, rows + 4, rows + 2
    mixed_chunks, grad_chunks = chunks_of(mixed_rows), chunks_of(grad_rows)
    v1_refs, bufs = bufs[: len(mixed_chunks)], bufs[len(mixed_chunks) :]
    v2_refs, bufs = bufs[: len(grad_chunks)], bufs[len(grad_chunks) :]
    hg_refs, m_refs = bufs[: len(grad_chunks)], bufs[len(grad_chunks) :]

    tapf_ref[...] = jnp.zeros(tapf_ref.shape, F32)
    for tap_row in range(3):
        for tap_col in range(3):
            low = 16 * tap_col + lat * tap_row
            tapf_ref[low : low + lat, :] = taps_ref[3 * tap_row + tap_col].astype(F32)
    win_ref[...] = tapf_ref[...].astype(BF16)

    me = me_ref[0]
    inside_top = jnp.where(me == 0, 0.0, 1.0).astype(F32)
    inside_bottom = jnp.where(me == parts - 1, 0.0, 1.0).astype(F32)
    root_a, root_b = roots(table_ref, step_ref[0])
    total = blocks[0][...].astype(F32)
    for block in blocks[1:]:
        total = total + block[...].astype(F32)
    latent = (total / root_a).astype(BF16)
    lat_rows = (rows + 2 * HALO) * lat
    for tap_col in range(3):
        lat_ref[tap_col, 0:lat_rows, :] = dot(latent, gather_ref[tap_col], 1, 0)
        lat_ref[tap_col, lat_rows:, :] = jnp.zeros((8, cols), F32)

    def edge(row, margin, total_rows, value):
        if row < margin:
            return value * inside_top
        if row >= total_rows - margin:
            return value * inside_bottom
        return value

    def spans(low, step=None):
        step = step or LANES
        return slice(low, min(low + step, chans))

    def put_planes(cells, row, chunks, targets, lanes):
        for plane, value in enumerate(to_planes(cells)):
            value = value.astype(BF16)
            for (low, high), target in zip(chunks, targets):
                if low <= row < high + 2:
                    target[plane, (row - low) * tiles : (row - low + 1) * tiles, lanes] = value

    def hidden_piece(row, lanes):
        def run():
            window = jnp.concatenate(
                [lat_ref[tap_col, lat * row : lat * row + 16, :] for tap_col in range(3)], axis=0
            ).astype(BF16)
            pre = dot(window, win_ref[:, lanes], 0, 0) + bin_ref[:, lanes]
            sig = 0.5 + 0.5 * jnp.tanh(0.5 * pre)
            act = pre * sig
            if 2 <= row < 2 + grad_rows:
                slope_ref[(row - 2) * cols : (row - 1) * cols, lanes] = (
                    sig + act * (1.0 - sig)
                ).astype(BF16)
            act = edge(row, 3, hidden_rows, act)
            cells = [act[part * tiles : (part + 1) * tiles] for part in range(TILE)]
            put_planes(cells, row, mixed_chunks, v1_refs, lanes)

        return run

    def mixed_piece(buf, row, base, lanes):
        def run():
            span = slice((row - base) * tiles, (row - base + 1) * tiles)
            cells = from_planes(*[buf[plane, span, lanes] for plane in range(6)])
            grads = []
            for cell in cells:
                pre = cell + bmid_ref[:, lanes]
                sig = 0.5 + 0.5 * jnp.tanh(0.5 * pre)
                grad = head_ref[:, lanes] * (sig * (1.0 + pre * (1.0 - sig)))
                grads.append(edge(row, 2, mixed_rows, grad))
            put_planes(grads, row, grad_chunks, v2_refs, lanes)

        return run

    def grad_piece(buf, row, base, target, lanes):
        def run():
            span = slice((row - base) * tiles, (row - base + 1) * tiles)
            cells = from_planes_back(*[buf[plane, span, lanes] for plane in range(6)])
            for part, cell in enumerate(cells):
                low = row * cols + part * tiles
                value = edge(row, 1, grad_rows, cell * slope_ref[low : low + tiles, lanes].astype(F32))
                low = (row - base) * cols + part * tiles
                target[low : low + tiles, lanes] = value.astype(BF16)

        return run

    def back_piece(row, base, target):
        def run():
            taps = dot(win_ref[...], target[(row - base) * cols : (row - base + 1) * cols], 1, 1)
            for tap_col in range(3):
                part = taps[16 * tap_col : 16 * tap_col + 16]
                high = part.astype(BF16)
                rest = (part - high.astype(F32)).astype(BF16)
                span = slice(tap_col * cols, (tap_col + 1) * cols)
                high_ref[16 * row : 16 * row + 16, span] = high
                rest_ref[16 * row : 16 * row + 16, span] = rest

        return run

    lane_parts = [spans(low) for low in range(0, chans, LANES)]
    queue = []
    for row in range(hidden_rows):
        queue += [(("hidden", row), -1, hidden_piece(row, lanes)) for lanes in lane_parts]
    for number, (low, high) in enumerate(mixed_chunks):
        buf = m_refs[number % len(m_refs)]
        for row in range(low, high):
            queue += [
                (("mixed", row), number, mixed_piece(buf, row, low, lanes)) for lanes in lane_parts
            ]
    for index, (low, high) in enumerate(grad_chunks):
        number = len(mixed_chunks) + index
        buf, target = m_refs[number % len(m_refs)], hg_refs[index]
        for row in range(low, high):
            queue += [
                (("grad", row), number, grad_piece(buf, row, low, target, lanes))
                for lanes in lane_parts
            ]
            queue.append((("back", row), number, back_piece(row, low, target)))
    queue.reverse()

    def flush(needed):
        while any(needed(item) for item in queue):
            queue.pop()[2]()

    def conv(step, chunk, source, back):
        low, high = chunk
        count = (high - low) * tiles
        buf = m_refs[step % len(m_refs)]
        for plane in (0, 5, 1, 2, 3, 4):
            kerns = []
            for shift in range(3):
                tap_row = 2 - shift if back else shift
                if plane in (0, 5):
                    first = (plane == 0) != back
                    kerns.append(wmid_ref[3 * tap_row + (0 if first else 2)])
                else:
                    which = (plane - 1) ^ 2 if back else plane - 1
                    kerns.append(planes_ref[which, tap_row])
            lhs = jnp.concatenate(
                [source[plane, shift * tiles : shift * tiles + count, :] for shift in range(3)], axis=1
            )
            buf[plane, 0:count, :] = dot(
                lhs, jnp.concatenate(kerns, axis=0 if back else 1), 1, 0 if back else 1
            )
            budget = QUOTA
            while budget > 0 and queue and queue[-1][1] < step:
                budget -= {"hidden": 1.0, "mixed": 1.0, "grad": 0.5, "back": 0.5}[queue[-1][0][0]]
                queue.pop()[2]()

    step = 0
    for chunk, source in zip(mixed_chunks, v1_refs):
        reach = chunk[1] + 2
        flush(lambda item: item[0][0] == "hidden" and item[0][1] < reach)
        flush(lambda item: 0 <= item[1] <= step - len(m_refs))
        conv(step, chunk, source, False)
        step += 1
    for chunk, source in zip(grad_chunks, v2_refs):
        reach = chunk[1] + 2
        flush(lambda item: item[0][0] == "mixed" and item[0][1] < reach)
        flush(lambda item: 0 <= item[1] <= step - len(m_refs))
        conv(step, chunk, source, True)
        step += 1
    flush(lambda item: True)

    q_ref[...] = dot(high_ref[...], scatter_ref[...], 1, 0) + dot(
        rest_ref[...], scatter_ref[...], 1, 0
    )
    for row in range(rows):
        lg_ref[lat * row : lat * row + lat, :] = (
            q_ref[16 * (row + 2) : 16 * (row + 2) + lat, :]
            + q_ref[16 * (row + 1) + lat : 16 * (row + 1) + 2 * lat, :]
            + q_ref[16 * row + 2 * lat : 16 * row + 3 * lat, :]
        )
    out_ref[...] = (-(root_b / root_a) * lg_ref[...]).astype(BF16)


def fill_windows(noise_ref, win_ref, lat):
    tall, cols = noise_ref.shape
    noise = noise_ref[...].astype(F32)
    spot = lax.broadcasted_iota(jnp.int32, (tall, cols), 1)
    none = jnp.zeros((lat, cols), F32)
    moved = (
        jnp.where(spot == cols - 1, 0.0, pltpu.roll(noise, cols - 1, 1)),
        noise,
        jnp.where(spot == 0, 0.0, pltpu.roll(noise, 1, 1)),
    )
    for tap_col in range(3):
        win_ref[tap_col, 0:lat, :] = none
        win_ref[tap_col, lat : lat + tall, :] = moved[tap_col]
        win_ref[tap_col, lat + tall :, :] = none


def window_of(win_ref, block, lat):
    group = (BLOCK + 2) * lat
    parts = []
    for low in range(block * WIDE * lat, (block + 1) * WIDE * lat, BLOCK * lat):
        parts.append(
            jnp.concatenate(
                [win_ref[tap_col, low : low + group, :] for tap_col in range(3)], axis=0
            )
        )
    return jnp.concatenate(parts, axis=1).astype(BF16)


def weight_kernel(
    noise_ref, thirds_ref, collect_ref, out_row_ref, in_row_ref, feat_ref, out_ref, win_ref, *, lat
):
    channels, height, _ = feat_ref.shape
    fill_windows(noise_ref, win_ref, lat)
    pairs = range(height // WIDE)
    feats = jnp.concatenate([pair_of(feat_ref, pair) for pair in pairs], axis=1)
    windows = jnp.concatenate([window_of(win_ref, pair, lat) for pair in pairs], axis=1)
    total = dot(feats, windows, 1, 1)
    gap = in_row_ref[...] - out_row_ref[...]
    kept = jnp.where((gap >= -2) & (gap <= 0), total, 0.0).astype(BF16)
    thirds = dot(thirds_ref[...], kept, 1, 0).astype(BF16)
    result = jnp.zeros(out_ref.shape, F32)
    for third in range(3):
        piece = thirds[third * channels : (third + 1) * channels]
        result = result + dot(collect_ref[third], piece, 1, 1)
    out_ref[...] = result


def feature_kernel(band_ref, noise_ref, out_ref, win_ref, *, lat):
    channels, _, cols = out_ref.shape
    pair = pl.program_id(0)

    @pl.when(pair == 0)
    def _():
        fill_windows(noise_ref, win_ref, lat)

    group = (BLOCK + 2) * lat
    parts = []
    for half in range(WIDE // BLOCK):
        low = pl.multiple_of((pair * WIDE + half * BLOCK) * lat, 8)
        parts.append(
            jnp.concatenate([win_ref[tap_col, pl.ds(low, group), :] for tap_col in range(3)], axis=0)
        )
    value = dot(band_ref[...], jnp.concatenate(parts, axis=1).astype(BF16), 1, 0).astype(BF16)
    for half in range(WIDE // BLOCK):
        out_ref[:, half * BLOCK : (half + 1) * BLOCK, :] = value[
            :, half * cols : (half + 1) * cols
        ].reshape(channels, BLOCK, cols)


VMEM = pl.BlockSpec(memory_space=pltpu.VMEM)
SMEM = pl.BlockSpec(memory_space=pltpu.SMEM)
ROOM = 2**20


def pinned(array):
    return pltpu.with_memory_space_constraint(jnp.asarray(array), pltpu.VMEM)


def from_hbm(array):
    return pltpu.with_memory_space_constraint(jnp.asarray(array), pltpu.HBM)


def call(kernel, scalars, operands, outs, scratch, name, left=(), room=24):
    return pl.pallas_call(
        kernel,
        in_specs=[SMEM] * len(scalars)
        + [VMEM] * len(operands)
        + [pl.BlockSpec(memory_space=pltpu.HBM)] * len(left),
        out_specs=jax.tree.map(lambda _: VMEM, outs),
        out_shape=outs,
        scratch_shapes=scratch,
        compiler_params=pltpu.CompilerParams(vmem_limit_bytes=room * ROOM),
        name=name,
    )(*scalars, *operands, *(from_hbm(one) for one in left))


def eps_call(step, me, feats, kern, noisy, parts, rows):
    channels, height, cols = feats.shape
    lat = noisy.shape[1]
    block_rows = (rows + 2 * HALO) * lat
    *blocks, band = call(
        functools.partial(eps_kernel, parts=parts, rows=rows, lat=lat),
        (step, me),
        (from_hbm(kern), from_hbm(noisy), from_hbm(schedule_table())),
        [pltpu.VMEM((block_rows, cols), BF16) for _ in range(parts)]
        + [pltpu.VMEM((3 * (BLOCK + 2) * lat, channels * BLOCK), BF16)],
        [
            pltpu.VMEM((channels, height, cols), BF16),
            pltpu.VMEM((3, (height + 2) * lat, cols), F32),
            pltpu.VMEM(((height + 2 * HALO) * lat, cols), F32),
            pltpu.VMEM((rows * lat, cols), F32),
            pltpu.SemaphoreType.DMA((height // WIDE,)),
        ],
        "eps_partial",
        (feats,),
    )
    return blocks, band


def prep_call(w_mid, band):
    chans = w_mid.shape[1]
    return call(
        prep_kernel,
        (),
        (pinned(band),),
        [pltpu.VMEM((4, 3, chans, chans), BF16), pltpu.VMEM(w_mid.shape, BF16),
         pltpu.VMEM(band.shape[::-1], BF16)],
        [pltpu.SemaphoreType.DMA((9,))],
        "weight_planes",
        (w_mid,),
    )


def decoder_call(step, me, moved, taps, b_in, b_mid, head, w_mid, planes, rows):
    lat, chans = taps.shape[1:]
    block_rows, cols = moved[0].shape
    tiles = cols // TILE
    gather, scatter = (jnp.asarray(part, BF16) for part in column_tables(cols))
    mixed_chunks, grad_chunks = chunks_of(rows + 4), chunks_of(rows + 2)
    tall_rows = [(high - low + 2) * tiles for low, high in mixed_chunks]
    back_rows = [(high - low + 2) * tiles for low, high in grad_chunks]
    return call(
        functools.partial(decoder_kernel, parts=len(moved), rows=rows, lat=lat, cols=cols),
        (step, me),
        tuple(pinned(one) for one in (
            *moved, schedule_table(), gather, scatter, taps, b_in[None, :], b_mid[None, :],
            head[None, :], w_mid, planes,
        )),
        jax.ShapeDtypeStruct((rows * lat, cols), BF16),
        [
            pltpu.VMEM((3, block_rows + 8, cols), F32),
            pltpu.VMEM(((rows + 2) * cols, chans), BF16),
            pltpu.VMEM(((rows + 2) * 16, 3 * cols), BF16),
            pltpu.VMEM(((rows + 2) * 16, 3 * cols), BF16),
            pltpu.VMEM(((rows + 2) * 16, cols), F32),
            pltpu.VMEM((rows * lat, cols), F32),
            pltpu.VMEM((48, chans), F32),
            pltpu.VMEM((48, chans), BF16),
        ]
        + [pltpu.VMEM((6, size, chans), BF16) for size in tall_rows + back_rows]
        + [pltpu.VMEM(((high - low) * cols, chans), BF16) for low, high in grad_chunks]
        + [pltpu.VMEM((6, CHUNK * tiles, chans), F32) for _ in range(3)],
        "decoder",
        room=46,
    )


def weight_call(feats, full, tables, lat):
    channels, height, cols = feats.shape
    return call(
        functools.partial(weight_kernel, lat=lat),
        (),
        (full, pinned(tables["thirds"]), pinned(tables["collect"]),
         pinned(tables["out_row"][None, :]), pinned(tables["in_row"][:, None]), pinned(feats)),
        jax.ShapeDtypeStruct((9 * lat, channels), F32),
        [pltpu.VMEM((3, (height + 2) * lat, cols), F32)],
        "weight_grad",
    )


def feature_call(band, full, channels, height, lat):
    cols = full.shape[1]
    return pl.pallas_call(
        functools.partial(feature_kernel, lat=lat),
        grid=(height // WIDE,),
        in_specs=[pl.BlockSpec(one.shape, lambda pair: (0, 0)) for one in (band, full)],
        out_specs=pl.BlockSpec((channels, WIDE, cols), lambda pair: (0, pair, 0)),
        out_shape=jax.ShapeDtypeStruct((channels, height, cols), BF16),
        scratch_shapes=[pltpu.VMEM((3, (height + 2) * lat, cols), F32)],
        compiler_params=pltpu.CompilerParams(vmem_limit_bytes=24 * ROOM),
        name="feature_grads",
    )(pinned(band), full)


def tables_of(channels, lat):
    names = ("out_row", "in_row", "thirds", "collect")
    tables = dict(zip(names, band_tables(channels, lat)))
    return {
        name: value if value.dtype == np.int32 else jnp.asarray(value, BF16)
        for name, value in tables.items()
    }


def body(features, w_out, noisy_latent, timestep, w_in, b_in, w_mid, b_mid, reward_head):
    _, channels, height, cols = features.shape
    lat, rows = noisy_latent.shape[1:3]
    parts, images = lax.axis_size("mp"), lax.axis_size("dp")
    feats, kern = features[0], w_out.T
    me = lax.axis_index("mp").astype(jnp.int32).reshape(1)
    tables = tables_of(channels, lat)
    blocks, band = eps_call(timestep, me, feats, kern, noisy_latent, parts, rows)
    moved = [blocks[0]] + [
        lax.ppermute(blocks[part], "mp", [(i, i ^ part) for i in range(parts)])
        for part in range(1, parts)
    ]
    planes, w_mid, band = prep_call(w_mid, band)
    taps = jnp.transpose(w_in, (0, 2, 1))
    noise = decoder_call(
        timestep, me, moved, taps, b_in, b_mid, reward_head, w_mid, planes, rows
    )
    full = lax.all_gather(noise, "mp", axis=0, tiled=True)
    weight_grad = weight_call(feats, full, tables, lat)
    stage = 1
    while stage < images:
        weight_grad = weight_grad + lax.ppermute(
            weight_grad, "dp", [(i, i ^ stage) for i in range(images)]
        )
        stage *= 2
    feature_grads = feature_call(band, full, channels, height, lat)
    return feature_grads[None], (weight_grad / (height * cols)).T


def solution(mesh):
    in_specs = (
        P("dp", "mp", None, None),
        P("mp", None),
        P("dp", None, "mp", None),
        P("dp"),
        P(),
        P(),
        P(),
        P(),
        P(),
    )
    out_specs = (P("dp", "mp", None, None), P("mp", None))
    return jax.shard_map(body, mesh=mesh, in_specs=in_specs, out_specs=out_specs, check_vma=False)
```

profile of v0, /device:TPU:0, one launch (start us, length us, event | category | flops | bytes accessed | tf_op | source)
XLA Modules:
  0.0 66.5 jit_solution(8392393770053906434)
XLA Ops:
  0.6 0.0 copy-start.7
  0.6 0.0 copy-start.3
  0.7 0.0 copy-start.4
  0.7 0.0 copy-start.10
  0.7 0.0 copy-start.9
  0.7 0.0 copy-start.8
  0.7 0.0 copy-start.6
  1.5 3.9 %eps_partial.1 = (bf16[160,128]{1,0:T(8,128)(2,1)S(1)}, bf16[160,128]{1,0:T(8,128)(2,1)S(1)}, bf16[160,128]{1,0:T(8,128)(2,1)S(1)}, bf16[160,128]{1,0:T(8,128)(2,1)S(1)}, bf16[216,1280]{1,0:T(8,128)(2,1)S(1)}) custom-call(s32[1]{0:T(128)S(6)} %copy.19.step_ref, s32[1]{0:T(128)} %bitcast.me_ref, bf16[36,80]{1,0:T(8,128)(2,1)} %bitcast.17, ...), custom_call_target="tpu_custom_call" | custom-call | tf_op jit(solution)/shard_map/eps_partial/pallas_call | solution.py:504
  5.3 0.5 collective-permute-start
  5.9 2.6 %collective-permute-start.1 = (bf16[160,128]{1,0:T(8,128)(2,1)S(1)}, bf16[160,128]{1,0:T(8,128)(2,1)S(1)}, u32[]{:S(2)}, u32[]{:S(2)}) collective-permute-start(bf16[160,128]{1,0:T(8,128)(2,1)S(1)} %get-tuple-element.14), channel_id=1, source_target_pairs={{0,2},{1,3},{2,0},{3,1},{4,6},{5,7},{6,4},{7,5},{8,10},{9,11},{10,... | collective-permute-start | bytes 122888 | tf_op jit(solution)/shard_map/ppermute | solution.py:633
  8.5 0.1 collective-permute-start.2
  8.5 3.5 %weight_planes.1 = (bf16[4,3,512,512]{3,2,1,0:T(8,128)(2,1)S(1)}, bf16[9,512,512]{2,1,0:T(8,128)(2,1)S(1)}, bf16[1280,216]{1,0:T(8,128)(2,1)S(1)}) custom-call(bf16[216,1280]{1,0:T(8,128)(2,1)S(1)} %get-tuple-element.10.band_ref, bf16[9,512,512]{2,1,0:T(8,128)(2,1)} %wmid_hbm.1), custom_call_target="tpu_custom_call" | custom-call | tf_op jit(solution)/shard_map/weight_planes/pallas_call | solution.py:504
  12.0 0.0 collective-permute-done.refs_1_
  12.0 0.0 collective-permute-done.1.refs_2_
  12.0 0.0 collective-permute-done.2.refs_3_
  12.1 0.0 copy-start
  12.1 0.0 copy-start.1
  12.1 0.0 copy-start.2
  12.2 0.0 copy-start.5
  12.2 0.0 copy-start.11
  12.2 33.4 %decoder.1 = bf16[128,128]{1,0:T(8,128)(2,1)} custom-call(s32[1]{0:T(128)S(6)} %copy.19.step_ref, s32[1]{0:T(128)} %bitcast.me_ref, bf16[160,128]{1,0:T(8,128)(2,1)S(1)} %get-tuple-element.12.refs_0_, bf16[160,128]{1,0:T(8,128)(2,1)S(1)} %collective-permute-done.refs_1_, bf16[160,128]{1,0:T(8,128)(2,1)S(1)} %collective-permute-done.1.refs_2_, ...), custom_call_target="tpu_custom_call" | custom-call | tf_op jit(solution)/shard_map/decoder/pallas_call | solution.py:504
  45.6 5.6 %all_gather.3.noise_ref = bf16[512,128]{1,0:T(8,128)(2,1)S(1)} all-gather(bf16[128,128]{1,0:T(8,128)(2,1)} %decoder.1), channel_id=1, replica_groups=mesh['dp'=8,'mp'=4] {'mp'}, dimensions={0}, use_global_device_ids=true | all-gather | bytes 163840 | tf_op jit(solution)/shard_map/all_gather | solution.py:641
  51.2 0.0 copy-done.1
  51.2 1.5 %weight_grad.1 = f32[36,80]{1,0:T(8,128)S(1)} custom-call(bf16[512,128]{1,0:T(8,128)(2,1)S(1)} %all_gather.3.noise_ref, bf16[240,1280]{1,0:T(8,128)(2,1)S(1)} %copy-done.2, bf16[3,36,216]{2,1,0:T(8,128)(2,1)S(1)} %copy-done.5, s32[1,216]{1,0:T(1,128)S(1)} %copy-done.11, s32[1280,1]{1,0:T(8,128)S(1)} %copy-done.1, bf16[80,128,128]{2,1,0:T(8,128)(2,1)S(1)} %bitcast.11), custom_call_target="tpu_custom_call" | custom-call | tf_op jit(solution)/shard_map/weight_grad/pallas_call | solution.py:504
  52.7 1.7 %collective-permute-start.3 = (f32[36,80]{1,0:T(8,128)S(1)}, f32[36,80]{1,0:T(8,128)S(1)}, u32[]{:S(2)}, u32[]{:S(2)}) collective-permute-start(f32[36,80]{1,0:T(8,128)S(1)} %weight_grad.1), channel_id=1, source_target_pairs={{0,4},{4,0},{8,12},{12,8},{16,20},{20,16},{24,28},{28,24},{1,5},{5... | collective-permute-start | bytes 34568 | tf_op jit(solution)/shard_map/ppermute | solution.py:645
  54.4 2.1 %collective-permute-done.3 = f32[36,80]{1,0:T(8,128)S(1)} collective-permute-done((f32[36,80]{1,0:T(8,128)S(1)}, f32[36,80]{1,0:T(8,128)S(1)}, u32[]{:S(2)}, u32[]{:S(2)}) %collective-permute-start.3) | collective-permute-done | bytes 11552 | tf_op jit(solution)/shard_map/ppermute | solution.py:645
  56.5 1.8 %collective-permute-start.4 = (f32[36,80]{1,0:T(8,128)S(1)}, f32[36,80]{1,0:T(8,128)S(1)}, u32[]{:S(2)}, u32[]{:S(2)}) collective-permute-start(f32[36,80]{1,0:T(8,128)S(1)} %add.9), channel_id=1, source_target_pairs={{0,8},{4,12},{8,0},{12,4},{16,24},{20,28},{24,16},{28,20},{1,9},{5... | collective-permute-start | bytes 34568 | tf_op jit(solution)/shard_map/ppermute | solution.py:645
  58.3 2.0 %collective-permute-done.4 = f32[36,80]{1,0:T(8,128)S(1)} collective-permute-done((f32[36,80]{1,0:T(8,128)S(1)}, f32[36,80]{1,0:T(8,128)S(1)}, u32[]{:S(2)}, u32[]{:S(2)}) %collective-permute-start.4) | collective-permute-done | bytes 11552 | tf_op jit(solution)/shard_map/ppermute | solution.py:645
  60.3 2.8 %collective-permute-start.5 = (f32[36,80]{1,0:T(8,128)S(1)}, f32[36,80]{1,0:T(8,128)S(1)}, u32[]{:S(2)}, u32[]{:S(2)}) collective-permute-start(f32[36,80]{1,0:T(8,128)S(1)} %add.10), channel_id=1, source_target_pairs={{0,16},{4,20},{8,24},{12,28},{16,0},{20,4},{24,8},{28,12},{1,17},{... | collective-permute-start | bytes 34568 | tf_op jit(solution)/shard_map/ppermute | solution.py:645
  63.1 2.8 %feature_grads.1 = bf16[80,128,128]{2,1,0:T(8,128)(2,1)} custom-call(bf16[1280,216]{1,0:T(8,128)(2,1)S(1)} %get-tuple-element.11.band_ref, bf16[512,128]{1,0:T(8,128)(2,1)S(1)} %all_gather.3.noise_ref), custom_call_target="tpu_custom_call" | custom-call | tf_op jit(solution)/shard_map/feature_grads/pallas_call | solution.py:603
  65.9 0.0 collective-permute-done.5
  65.9 0.6 multiply_bitcast_fusion
  (13 shorter events, 0.0 us)
Async XLA Ops:
  0.6 11.4 %copy-start.7 = (f32[8,128]{1,0:T(8,128)S(1)}, f32[8,128]{1,0:T(8,128)}, u32[]{:S(2)}) copy-start(f32[8,128]{1,0:T(8,128)} %constant.23.clone.table_ref.refs_4_) | copy-start | bytes 12292
  0.6 11.4 %copy-start.3 = (bf16[384,128]{1,0:T(8,128)(2,1)S(1)}, bf16[384,128]{1,0:T(8,128)(2,1)}, u32[]{:S(2)}) copy-start(bf16[384,128]{1,0:T(8,128)(2,1)} %constant.25.clone.refs_6_) | copy-start | bytes 294916
  0.7 11.4 %copy-start.4 = (bf16[3,128,128]{2,1,0:T(8,128)(2,1)S(1)}, bf16[3,128,128]{2,1,0:T(8,128)(2,1)}, u32[]{:S(2)}) copy-start(bf16[3,128,128]{2,1,0:T(8,128)(2,1)} %constant.24.clone.refs_5_) | copy-start | bytes 294916
  0.7 11.4 %copy-start.10 = (f32[512]{0:T(512)S(1)}, f32[512]{0:T(512)}, u32[]{:S(2)}) copy-start(f32[512]{0:T(512)} %param.25) | copy-start | bytes 6148
  0.7 11.4 %copy-start.9 = (f32[512]{0:T(512)S(1)}, f32[512]{0:T(512)}, u32[]{:S(2)}) copy-start(f32[512]{0:T(512)} %param.24) | copy-start | bytes 6148
  0.7 11.4 %copy-start.8 = (f32[512]{0:T(512)S(1)}, f32[512]{0:T(512)}, u32[]{:S(2)}) copy-start(f32[512]{0:T(512)} %param.22) | copy-start | bytes 6148
  0.7 11.4 %copy-start.6 = (bf16[9,512,4]{1,2,0:T(4,128)(2,1)S(1)}, bf16[9,512,4]{1,2,0:T(4,128)(2,1)}, u32[]{:S(2)}) copy-start(bf16[9,512,4]{1,2,0:T(4,128)(2,1)} %param.21) | copy-start | bytes 110596
  5.3 6.7 %collective-permute-start = (bf16[160,128]{1,0:T(8,128)(2,1)S(1)}, bf16[160,128]{1,0:T(8,128)(2,1)S(1)}, u32[]{:S(2)}, u32[]{:S(2)}) collective-permute-start(bf16[160,128]{1,0:T(8,128)(2,1)S(1)} %get-tuple-element.13), channel_id=1, source_target_pairs={{0,1},{1,0},{2,3},{3,2},{4,5},{5,4},{6,7},{7,6},{8,9},{9,8},{10,11... | collective-permute-start | bytes 122888 | tf_op jit(solution)/shard_map/ppermute | solution.py:633
  5.9 6.2 %collective-permute-start.1 = (bf16[160,128]{1,0:T(8,128)(2,1)S(1)}, bf16[160,128]{1,0:T(8,128)(2,1)S(1)}, u32[]{:S(2)}, u32[]{:S(2)}) collective-permute-start(bf16[160,128]{1,0:T(8,128)(2,1)S(1)} %get-tuple-element.14), channel_id=1, source_target_pairs={{0,2},{1,3},{2,0},{3,1},{4,6},{5,7},{6,4},{7,5},{8,10},{9,11},{10,... | collective-permute-start | bytes 122888 | tf_op jit(solution)/shard_map/ppermute | solution.py:633
  8.5 3.6 %collective-permute-start.2 = (bf16[160,128]{1,0:T(8,128)(2,1)S(1)}, bf16[160,128]{1,0:T(8,128)(2,1)S(1)}, u32[]{:S(2)}, u32[]{:S(2)}) collective-permute-start(bf16[160,128]{1,0:T(8,128)(2,1)S(1)} %get-tuple-element.15), channel_id=1, source_target_pairs={{0,3},{1,2},{2,1},{3,0},{4,7},{5,6},{6,5},{7,4},{8,11},{9,10},{10,... | collective-permute-start | bytes 122888 | tf_op jit(solution)/shard_map/ppermute | solution.py:633
  12.1 39.1 %copy-start = (bf16[1,80,128,128]{3,2,1,0:T(8,128)(2,1)S(1)}, bf16[1,80,128,128]{3,2,1,0:T(8,128)(2,1)}, u32[]{:S(2)}) copy-start(bf16[1,80,128,128]{3,2,1,0:T(8,128)(2,1)} %param.17) | copy-start | bytes 7864324
  12.1 39.1 %copy-start.1 = (s32[1280,1]{1,0:T(8,128)S(1)}, s32[1280,1]{1,0:T(8,128)}, u32[]{:S(2)}) copy-start(s32[1280,1]{1,0:T(8,128)} %constant.27.clone.in_row_ref) | copy-start | bytes 15364
  12.1 39.1 %copy-start.2 = (bf16[240,1280]{1,0:T(8,128)(2,1)S(1)}, bf16[240,1280]{1,0:T(8,128)(2,1)}, u32[]{:S(2)}) copy-start(bf16[240,1280]{1,0:T(8,128)(2,1)} %constant.21.clone.thirds_ref) | copy-start | bytes 1843204
  12.2 39.1 %copy-start.5 = (bf16[3,36,216]{2,1,0:T(8,128)(2,1)S(1)}, bf16[3,36,216]{2,1,0:T(8,128)(2,1)}, u32[]{:S(2)}) copy-start(bf16[3,36,216]{2,1,0:T(8,128)(2,1)} %constant.22.clone.collect_ref) | copy-start | bytes 139972
  12.2 39.1 %copy-start.11 = (s32[1,216]{1,0:T(1,128)S(1)}, s32[1,216]{1,0:T(1,128)}, u32[]{:S(2)}) copy-start(s32[1,216]{1,0:T(1,128)} %constant.26.clone.out_row_ref) | copy-start | bytes 2596
  52.7 3.8 %collective-permute-start.3 = (f32[36,80]{1,0:T(8,128)S(1)}, f32[36,80]{1,0:T(8,128)S(1)}, u32[]{:S(2)}, u32[]{:S(2)}) collective-permute-start(f32[36,80]{1,0:T(8,128)S(1)} %weight_grad.1), channel_id=1, source_target_pairs={{0,4},{4,0},{8,12},{12,8},{16,20},{20,16},{24,28},{28,24},{1,5},{5... | collective-permute-start | bytes 34568 | tf_op jit(solution)/shard_map/ppermute | solution.py:645
  56.5 3.8 %collective-permute-start.4 = (f32[36,80]{1,0:T(8,128)S(1)}, f32[36,80]{1,0:T(8,128)S(1)}, u32[]{:S(2)}, u32[]{:S(2)}) collective-permute-start(f32[36,80]{1,0:T(8,128)S(1)} %add.9), channel_id=1, source_target_pairs={{0,8},{4,12},{8,0},{12,4},{16,24},{20,28},{24,16},{28,20},{1,9},{5... | collective-permute-start | bytes 34568 | tf_op jit(solution)/shard_map/ppermute | solution.py:645
  60.3 5.6 %collective-permute-start.5 = (f32[36,80]{1,0:T(8,128)S(1)}, f32[36,80]{1,0:T(8,128)S(1)}, u32[]{:S(2)}, u32[]{:S(2)}) collective-permute-start(f32[36,80]{1,0:T(8,128)S(1)} %add.10), channel_id=1, source_target_pairs={{0,16},{4,20},{8,24},{12,28},{16,0},{20,4},{24,8},{28,12},{1,17},{... | collective-permute-start | bytes 34568 | tf_op jit(solution)/shard_map/ppermute | solution.py:645
where the time goes:
time: 66.8 us; the launch traced here: 66.5 us
  Pallas kernels  45 us (67%)
  starting transfers between devices  9.47 us (14%)
  blocking collectives  5.64 us (8%)
  waiting for transfers between devices  4.1 us (6%)
  between operations  1.6 us (2%)
    pallas_call x4, Pallas kernels, call(): pl.pallas_call(kernel, in_specs=[SMEM] * len(scalars) + [VMEM] * len(oper...  42.2 us
    ppermute x3, starting transfers between devices, body(): lax.ppermute(weight_grad, 'dp', [(i, i ^ stage) for i in range(images)])  6.29 us
    all_gather x1, blocking collectives, body(): full = lax.all_gather(noise, 'mp', axis=0, tiled=True)  5.64 us
    ppermute x3, waiting for transfers between devices, body(): lax.ppermute(weight_grad, 'dp', [(i, i ^ stage) for i in range(images)])  4.1 us
    ppermute x3, starting transfers between devices, body(): lax.ppermute(blocks[part], 'mp', [(i, i ^ part) for i in range(parts)])  3.18 us
    pallas_call x1, Pallas kernels, feature_call(): pl.pallas_call(functools.partial(feature_kernel, lat=lat), grid=(height /...  2.82 us
  transfers between devices with their start and end apart: 6, of which 2 were waited for; matrix products, arithmetic and copies ran while one was open for 0% of the time, Pallas kernels for 9%

commit v1 on v0

--- a/solution.py
+++ b/solution.py
@@ -15,10 +15,10 @@
 PT_A = 0.5**0.5
 PT_B = 2.0**0.5
 STEPS = 1000
-CHUNK = 9
+CHUNK = 18
 LANES = 256
 PREP_ROWS = 32
-QUOTA = 4.5
+QUOTA = 100.0
 F32 = jnp.float32
 BF16 = jnp.bfloat16
 
@@ -209,13 +209,14 @@
     )
 
 
-def from_planes(m0, ap, an, bp, bn, m5):
-    sum_a, dif_a, sum_b, dif_b = ap + an, PT_A * (ap - an), bp + bn, PT_B * (bp - bn)
+def half_from_planes(m0, ap, an, bp, bn, m5):
+    sum_a, dif_a = ap + an, (0.5 * PT_A) * (ap - an)
+    sum_b, dif_b = bp + bn, (0.5 * PT_B) * (bp - bn)
     return (
-        m0 + sum_a + sum_b,
+        0.5 * (m0 + sum_a + sum_b),
         dif_a + dif_b,
-        0.5 * sum_a + 2.0 * sum_b,
-        0.5 * dif_a + 2.0 * dif_b + m5,
+        0.25 * sum_a + sum_b,
+        0.5 * dif_a + 2.0 * dif_b + 0.5 * m5,
     )
 
 
@@ -251,7 +252,7 @@
         for tap_col in range(3):
             low = 16 * tap_col + lat * tap_row
             tapf_ref[low : low + lat, :] = taps_ref[3 * tap_row + tap_col].astype(F32)
-    win_ref[...] = tapf_ref[...].astype(BF16)
+    win_ref[...] = (0.5 * tapf_ref[...]).astype(BF16)
 
     me = me_ref[0]
     inside_top = jnp.where(me == 0, 0.0, 1.0).astype(F32)
@@ -289,12 +290,13 @@
             window = jnp.concatenate(
                 [lat_ref[tap_col, lat * row : lat * row + 16, :] for tap_col in range(3)], axis=0
             ).astype(BF16)
-            pre = dot(window, win_ref[:, lanes], 0, 0) + bin_ref[:, lanes]
-            sig = 0.5 + 0.5 * jnp.tanh(0.5 * pre)
-            act = pre * sig
+            half = dot(window, win_ref[:, lanes], 0, 0) + 0.5 * bin_ref[:, lanes]
+            tanh = jnp.tanh(half)
+            twice = 1.0 + tanh
+            act = half * twice
             if 2 <= row < 2 + grad_rows:
                 slope_ref[(row - 2) * cols : (row - 1) * cols, lanes] = (
-                    sig + act * (1.0 - sig)
+                    twice + act * (1.0 - tanh)
                 ).astype(BF16)
             act = edge(row, 3, hidden_rows, act)
             cells = [act[part * tiles : (part + 1) * tiles] for part in range(TILE)]
@@ -305,12 +307,13 @@
     def mixed_piece(buf, row, base, lanes):
         def run():
             span = slice((row - base) * tiles, (row - base + 1) * tiles)
-            cells = from_planes(*[buf[plane, span, lanes] for plane in range(6)])
+            cells = half_from_planes(*[buf[plane, span, lanes] for plane in range(6)])
             grads = []
             for cell in cells:
-                pre = cell + bmid_ref[:, lanes]
-                sig = 0.5 + 0.5 * jnp.tanh(0.5 * pre)
-                grad = head_ref[:, lanes] * (sig * (1.0 + pre * (1.0 - sig)))
+                half = cell + 0.5 * bmid_ref[:, lanes]
+                tanh = jnp.tanh(half)
+                twice = 1.0 + tanh
+                grad = (0.5 * head_ref[:, lanes]) * (twice + half * twice * (1.0 - tanh))
                 grads.append(edge(row, 2, mixed_rows, grad))
             put_planes(grads, row, grad_chunks, v2_refs, lanes)
 
@@ -465,11 +468,12 @@
     out_ref[...] = result
 
 
-def feature_kernel(band_ref, noise_ref, out_ref, win_ref, *, lat):
+def feature_kernel(band_ref, noise_ref, *refs, first, lat):
+    out_ref, win_ref = refs[-2:]
     channels, _, cols = out_ref.shape
-    pair = pl.program_id(0)
-
-    @pl.when(pair == 0)
+    pair = pl.program_id(0) + first
+
+    @pl.when(pl.program_id(0) == 0)
     def _():
         fill_windows(noise_ref, win_ref, lat)
 
@@ -598,18 +602,21 @@
     )
 
 
-def feature_call(band, full, channels, height, lat):
+def feature_call(band, full, channels, height, lat, first, last, before=None):
     cols = full.shape[1]
+    extra = [] if before is None else [before]
     return pl.pallas_call(
-        functools.partial(feature_kernel, lat=lat),
-        grid=(height // WIDE,),
-        in_specs=[pl.BlockSpec(one.shape, lambda pair: (0, 0)) for one in (band, full)],
-        out_specs=pl.BlockSpec((channels, WIDE, cols), lambda pair: (0, pair, 0)),
+        functools.partial(feature_kernel, first=first, lat=lat),
+        grid=(last - first,),
+        in_specs=[pl.BlockSpec(one.shape, lambda pair: (0, 0)) for one in (band, full)]
+        + [pl.BlockSpec(memory_space=pltpu.HBM) for _ in extra],
+        out_specs=pl.BlockSpec((channels, WIDE, cols), lambda pair: (0, pair + first, 0)),
         out_shape=jax.ShapeDtypeStruct((channels, height, cols), BF16),
         scratch_shapes=[pltpu.VMEM((3, (height + 2) * lat, cols), F32)],
+        input_output_aliases={2: 0} if extra else {},
         compiler_params=pltpu.CompilerParams(vmem_limit_bytes=24 * ROOM),
         name="feature_grads",
-    )(pinned(band), full)
+    )(pinned(band), full, *extra)
 
 
 def tables_of(channels, lat):
@@ -640,13 +647,18 @@
     )
     full = lax.all_gather(noise, "mp", axis=0, tiled=True)
     weight_grad = weight_call(feats, full, tables, lat)
-    stage = 1
+    pairs = height // WIDE
+    stage, feature_grads = 1, None
     while stage < images:
-        weight_grad = weight_grad + lax.ppermute(
-            weight_grad, "dp", [(i, i ^ stage) for i in range(images)]
-        )
+        other = lax.ppermute(weight_grad, "dp", [(i, i ^ stage) for i in range(images)])
+        if stage == 1:
+            feature_grads = feature_call(band, full, channels, height, lat, 0, pairs // 2)
+            other, feature_grads = lax.optimization_barrier((other, feature_grads))
+        weight_grad = weight_grad + other
         stage *= 2
-    feature_grads = feature_call(band, full, channels, height, lat)
+    feature_grads = feature_call(
+        band, full, channels, height, lat, pairs // 2, pairs, feature_grads
+    )
     return feature_grads[None], (weight_grad / (height * cols)).T
 
 

time: 66.8 us -> 65.1 us (0.975)
  waiting for transfers between devices: 4.1 us -> 2.7 us
    ppermute x3, waiting for transfers between devices: 4.1 us -> 2.7 us  [body(): lax.ppermute(weight_grad, 'dp', [(i, i ^ stage) for i in range(images)])]
    pallas_call x4, Pallas kernels: 42.2 us -> 41.5 us  [call(): pl.pallas_call(kernel, in_specs=[SMEM] * len(scalars) + [VMEM] * len(oper...]
    pallas_call x1 -> x2, Pallas kernels: 2.82 us -> 3.32 us  [feature_call(): pl.pallas_call(functools.partial(feature_kernel, first=first, lat=lat), g...]
  transfers between devices with their start and end apart: 6 -> 6, of which waited for: 2 -> 3; matrix products, arithmetic and copies ran while one was open for 0% -> 0% of each run, Pallas kernels for 9% -> 10%
where the time goes in v1:
time: 65.1 us; the launch traced here: 64.9 us
  Pallas kernels  44.9 us (69%)
  starting transfers between devices  9.44 us (15%)
  blocking collectives  5.64 us (9%)
  waiting for transfers between devices  2.7 us (4%)
  between operations  1.6 us (2%)
    pallas_call x4, Pallas kernels, call(): pl.pallas_call(kernel, in_specs=[SMEM] * len(scalars) + [VMEM] * len(oper...  41.5 us
    ppermute x3, starting transfers between devices, body(): lax.ppermute(weight_grad, 'dp', [(i, i ^ stage) for i in range(images)])  6.26 us
    all_gather x1, blocking collectives, body(): full = lax.all_gather(noise, 'mp', axis=0, tiled=True)  5.64 us
    pallas_call x2, Pallas kernels, feature_call(): pl.pallas_call(functools.partial(feature_kernel, first=first, lat=lat), g...  3.32 us
    ppermute x3, starting transfers between devices, body(): lax.ppermute(blocks[part], 'mp', [(i, i ^ part) for i in range(parts)])  3.18 us
    ppermute x3, waiting for transfers between devices, body(): lax.ppermute(weight_grad, 'dp', [(i, i ^ stage) for i in range(images)])  2.7 us
  transfers between devices with their start and end apart: 6, of which 3 were waited for; matrix products, arithmetic and copies ran while one was open for 0% of the time, Pallas kernels for 10%

profile of v1, /device:TPU:0, one launch (start us, length us, event | category | flops | bytes accessed | tf_op | source)
XLA Modules:
  0.0 64.9 jit_solution(5387990271715160019)
XLA Ops:
  0.6 0.0 copy-start.7
  0.6 0.0 copy-start.3
  0.7 0.0 copy-start.4
  0.7 0.0 copy-start.10
  0.7 0.0 copy-start.9
  0.7 0.0 copy-start.8
  1.5 3.9 %eps_partial.1 = (bf16[160,128]{1,0:T(8,128)(2,1)S(1)}, bf16[160,128]{1,0:T(8,128)(2,1)S(1)}, bf16[160,128]{1,0:T(8,128)(2,1)S(1)}, bf16[160,128]{1,0:T(8,128)(2,1)S(1)}, bf16[216,1280]{1,0:T(8,128)(2,1)S(1)}) custom-call(s32[1]{0:T(128)S(6)} %copy.21.step_ref, s32[1]{0:T(128)} %bitcast.me_ref, bf16[36,80]{1,0:T(8,128)(2,1)} %bitcast.17, ...), custom_call_target="tpu_custom_call" | custom-call | tf_op jit(solution)/shard_map/eps_partial/pallas_call | solution.py:508
  5.3 0.5 collective-permute-start
  5.9 2.6 %collective-permute-start.1 = (bf16[160,128]{1,0:T(8,128)(2,1)S(1)}, bf16[160,128]{1,0:T(8,128)(2,1)S(1)}, u32[]{:S(2)}, u32[]{:S(2)}) collective-permute-start(bf16[160,128]{1,0:T(8,128)(2,1)S(1)} %get-tuple-element.16), channel_id=1, source_target_pairs={{0,2},{1,3},{2,0},{3,1},{4,6},{5,7},{6,4},{7,5},{8,10},{9,11},{10,... | collective-permute-start | bytes 122888 | tf_op jit(solution)/shard_map/ppermute | solution.py:640
  8.5 0.1 collective-permute-start.2
  8.5 3.5 %weight_planes.1 = (bf16[4,3,512,512]{3,2,1,0:T(8,128)(2,1)S(1)}, bf16[9,512,512]{2,1,0:T(8,128)(2,1)S(1)}, bf16[1280,216]{1,0:T(8,128)(2,1)S(1)}) custom-call(bf16[216,1280]{1,0:T(8,128)(2,1)S(1)} %get-tuple-element.12.band_ref, bf16[9,512,512]{2,1,0:T(8,128)(2,1)} %wmid_hbm.1), custom_call_target="tpu_custom_call" | custom-call | tf_op jit(solution)/shard_map/weight_planes/pallas_call | solution.py:508
  12.0 0.0 collective-permute-done.refs_1_
  12.0 0.0 collective-permute-done.1.refs_2_
  12.0 0.0 collective-permute-done.2.refs_3_
  12.1 0.0 copy-start
  12.1 0.0 copy-start.1
  12.1 0.0 copy-start.2
  12.2 0.0 copy-start.5
  12.2 0.0 copy-start.11
  12.2 32.7 %decoder.1 = bf16[128,128]{1,0:T(8,128)(2,1)} custom-call(s32[1]{0:T(128)S(6)} %copy.21.step_ref, s32[1]{0:T(128)} %bitcast.me_ref, bf16[160,128]{1,0:T(8,128)(2,1)S(1)} %get-tuple-element.14.refs_0_, bf16[160,128]{1,0:T(8,128)(2,1)S(1)} %collective-permute-done.refs_1_, bf16[160,128]{1,0:T(8,128)(2,1)S(1)} %collective-permute-done.1.refs_2_, ...), custom_call_target="tpu_custom_call" | custom-call | tf_op jit(solution)/shard_map/decoder/pallas_call | solution.py:508
  44.9 5.6 %all_gather.3.noise_ref = bf16[512,128]{1,0:T(8,128)(2,1)S(1)} all-gather(bf16[128,128]{1,0:T(8,128)(2,1)} %decoder.1), channel_id=1, replica_groups=mesh['dp'=8,'mp'=4] {'mp'}, dimensions={0}, use_global_device_ids=true | all-gather | bytes 163840 | tf_op jit(solution)/shard_map/all_gather | solution.py:648
  50.5 0.0 copy-done
  50.5 1.5 %weight_grad.1 = f32[36,80]{1,0:T(8,128)S(1)} custom-call(bf16[512,128]{1,0:T(8,128)(2,1)S(1)} %all_gather.3.noise_ref, bf16[240,1280]{1,0:T(8,128)(2,1)S(1)} %copy-done.2, bf16[3,36,216]{2,1,0:T(8,128)(2,1)S(1)} %copy-done.5, s32[1,216]{1,0:T(1,128)S(1)} %copy-done.11, s32[1280,1]{1,0:T(8,128)S(1)} %copy-done.1, bf16[80,128,128]{2,1,0:T(8,128)(2,1)S(1)} %bitcast.11), custom_call_target="tpu_custom_call" | custom-call | tf_op jit(solution)/shard_map/weight_grad/pallas_call | solution.py:508
  52.0 1.7 %collective-permute-start.3 = (f32[36,80]{1,0:T(8,128)S(1)}, f32[36,80]{1,0:T(8,128)S(1)}, u32[]{:S(2)}, u32[]{:S(2)}) collective-permute-start(f32[36,80]{1,0:T(8,128)S(1)} %weight_grad.1), channel_id=1, source_target_pairs={{0,4},{4,0},{8,12},{12,8},{16,20},{20,16},{24,28},{28,24},{1,5},{5... | collective-permute-start | bytes 34568 | tf_op jit(solution)/shard_map/ppermute | solution.py:653
  53.7 1.7 %feature_grads.2.refs_0_ = bf16[80,128,128]{2,1,0:T(8,128)(2,1)} custom-call(bf16[1280,216]{1,0:T(8,128)(2,1)S(1)} %get-tuple-element.13.band_ref, bf16[512,128]{1,0:T(8,128)(2,1)S(1)} %all_gather.3.noise_ref), custom_call_target="tpu_custom_call" | custom-call | tf_op jit(solution)/shard_map/feature_grads/pallas_call | solution.py:608
  55.4 0.4 collective-permute-done.3
  55.8 1.8 %collective-permute-start.4 = (f32[36,80]{1,0:T(8,128)S(1)}, f32[36,80]{1,0:T(8,128)S(1)}, u32[]{:S(2)}, u32[]{:S(2)}) collective-permute-start(f32[36,80]{1,0:T(8,128)S(1)} %add.9), channel_id=1, source_target_pairs={{0,8},{4,12},{8,0},{12,4},{16,24},{20,28},{24,16},{28,20},{1,9},{5... | collective-permute-start | bytes 34568 | tf_op jit(solution)/shard_map/ppermute | solution.py:653
  57.6 2.0 %collective-permute-done.4 = f32[36,80]{1,0:T(8,128)S(1)} collective-permute-done((f32[36,80]{1,0:T(8,128)S(1)}, f32[36,80]{1,0:T(8,128)S(1)}, u32[]{:S(2)}, u32[]{:S(2)}) %collective-permute-start.4) | collective-permute-done | bytes 11552 | tf_op jit(solution)/shard_map/ppermute | solution.py:653
  59.6 2.8 %collective-permute-start.5 = (f32[36,80]{1,0:T(8,128)S(1)}, f32[36,80]{1,0:T(8,128)S(1)}, u32[]{:S(2)}, u32[]{:S(2)}) collective-permute-start(f32[36,80]{1,0:T(8,128)S(1)} %add.10), channel_id=1, source_target_pairs={{0,16},{4,20},{8,24},{12,28},{16,0},{20,4},{24,8},{28,12},{1,17},{... | collective-permute-start | bytes 34568 | tf_op jit(solution)/shard_map/ppermute | solution.py:653
  62.4 1.7 %feature_grads.3 = bf16[80,128,128]{2,1,0:T(8,128)(2,1)} custom-call(bf16[1280,216]{1,0:T(8,128)(2,1)S(1)} %get-tuple-element.13.band_ref, bf16[512,128]{1,0:T(8,128)(2,1)S(1)} %all_gather.3.noise_ref, bf16[80,128,128]{2,1,0:T(8,128)(2,1)} %feature_grads.2.refs_0_), custom_call_target="tpu_custom_call", output_to_operand_aliasing={{}: (2, {})} | custom-call | tf_op jit(solution)/shard_map/feature_grads/pallas_call | solution.py:608
  64.1 0.2 collective-permute-done.5
  64.3 0.6 multiply_bitcast_fusion
  (14 shorter events, 0.0 us)
Async XLA Ops:
  0.6 11.4 %copy-start.7 = (f32[8,128]{1,0:T(8,128)S(1)}, f32[8,128]{1,0:T(8,128)}, u32[]{:S(2)}) copy-start(f32[8,128]{1,0:T(8,128)} %constant.23.clone.table_ref.refs_4_) | copy-start | bytes 12292
  0.6 11.4 %copy-start.3 = (bf16[384,128]{1,0:T(8,128)(2,1)S(1)}, bf16[384,128]{1,0:T(8,128)(2,1)}, u32[]{:S(2)}) copy-start(bf16[384,128]{1,0:T(8,128)(2,1)} %constant.25.clone.refs_6_) | copy-start | bytes 294916
  0.7 11.4 %copy-start.4 = (bf16[3,128,128]{2,1,0:T(8,128)(2,1)S(1)}, bf16[3,128,128]{2,1,0:T(8,128)(2,1)}, u32[]{:S(2)}) copy-start(bf16[3,128,128]{2,1,0:T(8,128)(2,1)} %constant.24.clone.refs_5_) | copy-start | bytes 294916
  0.7 11.4 %copy-start.10 = (f32[512]{0:T(512)S(1)}, f32[512]{0:T(512)}, u32[]{:S(2)}) copy-start(f32[512]{0:T(512)} %param.25) | copy-start | bytes 6148
  0.7 11.4 %copy-start.9 = (f32[512]{0:T(512)S(1)}, f32[512]{0:T(512)}, u32[]{:S(2)}) copy-start(f32[512]{0:T(512)} %param.24) | copy-start | bytes 6148
  0.7 11.4 %copy-start.8 = (f32[512]{0:T(512)S(1)}, f32[512]{0:T(512)}, u32[]{:S(2)}) copy-start(f32[512]{0:T(512)} %param.22) | copy-start | bytes 6148
  0.7 11.4 %copy-start.6 = (bf16[9,512,4]{1,2,0:T(4,128)(2,1)S(1)}, bf16[9,512,4]{1,2,0:T(4,128)(2,1)}, u32[]{:S(2)}) copy-start(bf16[9,512,4]{1,2,0:T(4,128)(2,1)} %param.21) | copy-start | bytes 110596
  5.3 6.7 %collective-permute-start = (bf16[160,128]{1,0:T(8,128)(2,1)S(1)}, bf16[160,128]{1,0:T(8,128)(2,1)S(1)}, u32[]{:S(2)}, u32[]{:S(2)}) collective-permute-start(bf16[160,128]{1,0:T(8,128)(2,1)S(1)} %get-tuple-element.15), channel_id=1, source_target_pairs={{0,1},{1,0},{2,3},{3,2},{4,5},{5,4},{6,7},{7,6},{8,9},{9,8},{10,11... | collective-permute-start | bytes 122888 | tf_op jit(solution)/shard_map/ppermute | solution.py:640
  5.9 6.2 %collective-permute-start.1 = (bf16[160,128]{1,0:T(8,128)(2,1)S(1)}, bf16[160,128]{1,0:T(8,128)(2,1)S(1)}, u32[]{:S(2)}, u32[]{:S(2)}) collective-permute-start(bf16[160,128]{1,0:T(8,128)(2,1)S(1)} %get-tuple-element.16), channel_id=1, source_target_pairs={{0,2},{1,3},{2,0},{3,1},{4,6},{5,7},{6,4},{7,5},{8,10},{9,11},{10,... | collective-permute-start | bytes 122888 | tf_op jit(solution)/shard_map/ppermute | solution.py:640
  8.5 3.6 %collective-permute-start.2 = (bf16[160,128]{1,0:T(8,128)(2,1)S(1)}, bf16[160,128]{1,0:T(8,128)(2,1)S(1)}, u32[]{:S(2)}, u32[]{:S(2)}) collective-permute-start(bf16[160,128]{1,0:T(8,128)(2,1)S(1)} %get-tuple-element.17), channel_id=1, source_target_pairs={{0,3},{1,2},{2,1},{3,0},{4,7},{5,6},{6,5},{7,4},{8,11},{9,10},{10,... | collective-permute-start | bytes 122888 | tf_op jit(solution)/shard_map/ppermute | solution.py:640
  12.1 38.4 %copy-start = (bf16[1,80,128,128]{3,2,1,0:T(8,128)(2,1)S(1)}, bf16[1,80,128,128]{3,2,1,0:T(8,128)(2,1)}, u32[]{:S(2)}) copy-start(bf16[1,80,128,128]{3,2,1,0:T(8,128)(2,1)} %param.17) | copy-start | bytes 7864324
  12.1 38.4 %copy-start.1 = (s32[1280,1]{1,0:T(8,128)S(1)}, s32[1280,1]{1,0:T(8,128)}, u32[]{:S(2)}) copy-start(s32[1280,1]{1,0:T(8,128)} %constant.27.clone.in_row_ref) | copy-start | bytes 15364
  12.1 38.4 %copy-start.2 = (bf16[240,1280]{1,0:T(8,128)(2,1)S(1)}, bf16[240,1280]{1,0:T(8,128)(2,1)}, u32[]{:S(2)}) copy-start(bf16[240,1280]{1,0:T(8,128)(2,1)} %constant.21.clone.thirds_ref) | copy-start | bytes 1843204
  12.2 38.4 %copy-start.5 = (bf16[3,36,216]{2,1,0:T(8,128)(2,1)S(1)}, bf16[3,36,216]{2,1,0:T(8,128)(2,1)}, u32[]{:S(2)}) copy-start(bf16[3,36,216]{2,1,0:T(8,128)(2,1)} %constant.22.clone.collect_ref) | copy-start | bytes 139972
  12.2 38.4 %copy-start.11 = (s32[1,216]{1,0:T(1,128)S(1)}, s32[1,216]{1,0:T(1,128)}, u32[]{:S(2)}) copy-start(s32[1,216]{1,0:T(1,128)} %constant.26.clone.out_row_ref) | copy-start | bytes 2596
  52.0 3.8 %collective-permute-start.3 = (f32[36,80]{1,0:T(8,128)S(1)}, f32[36,80]{1,0:T(8,128)S(1)}, u32[]{:S(2)}, u32[]{:S(2)}) collective-permute-start(f32[36,80]{1,0:T(8,128)S(1)} %weight_grad.1), channel_id=1, source_target_pairs={{0,4},{4,0},{8,12},{12,8},{16,20},{20,16},{24,28},{28,24},{1,5},{5... | collective-permute-start | bytes 34568 | tf_op jit(solution)/shard_map/ppermute | solution.py:653
  55.8 3.8 %collective-permute-start.4 = (f32[36,80]{1,0:T(8,128)S(1)}, f32[36,80]{1,0:T(8,128)S(1)}, u32[]{:S(2)}, u32[]{:S(2)}) collective-permute-start(f32[36,80]{1,0:T(8,128)S(1)} %add.9), channel_id=1, source_target_pairs={{0,8},{4,12},{8,0},{12,4},{16,24},{20,28},{24,16},{28,20},{1,9},{5... | collective-permute-start | bytes 34568 | tf_op jit(solution)/shard_map/ppermute | solution.py:653
  59.6 4.7 %collective-permute-start.5 = (f32[36,80]{1,0:T(8,128)S(1)}, f32[36,80]{1,0:T(8,128)S(1)}, u32[]{:S(2)}, u32[]{:S(2)}) collective-permute-start(f32[36,80]{1,0:T(8,128)S(1)} %add.10), channel_id=1, source_target_pairs={{0,16},{4,20},{8,24},{12,28},{16,0},{20,4},{24,8},{28,12},{1,17},{... | collective-permute-start | bytes 34568 | tf_op jit(solution)/shard_map/ppermute | solution.py:653

commit v2 on v1

--- a/solution.py
+++ b/solution.py
@@ -285,12 +285,22 @@
                 if low <= row < high + 2:
                     target[plane, (row - low) * tiles : (row - low + 1) * tiles, lanes] = value
 
-    def hidden_piece(row, lanes):
+    def hidden_matmul(buf, plane, rows_in):
         def run():
-            window = jnp.concatenate(
-                [lat_ref[tap_col, lat * row : lat * row + 16, :] for tap_col in range(3)], axis=0
-            ).astype(BF16)
-            half = dot(window, win_ref[:, lanes], 0, 0) + 0.5 * bin_ref[:, lanes]
+            windows = [
+                jnp.concatenate(
+                    [lat_ref[tap_col, lat * row : lat * row + 16, :] for tap_col in range(3)], axis=0
+                )
+                for row in rows_in
+            ]
+            windows = jnp.concatenate(windows, axis=1).astype(BF16)
+            buf[plane, 0 : len(rows_in) * cols, :] = dot(windows, win_ref[...], 0, 0)
+
+        return run
+
+    def hidden_piece(buf, plane, spot, row, lanes):
+        def run():
+            half = buf[plane, spot * cols : (spot + 1) * cols, lanes] + 0.5 * bin_ref[:, lanes]
             tanh = jnp.tanh(half)
             twice = 1.0 + tanh
             act = half * twice
@@ -331,23 +341,36 @@
 
         return run
 
-    def back_piece(row, base, target):
+    def back_piece(low, high, target):
         def run():
-            taps = dot(win_ref[...], target[(row - base) * cols : (row - base + 1) * cols], 1, 1)
-            for tap_col in range(3):
-                part = taps[16 * tap_col : 16 * tap_col + 16]
-                high = part.astype(BF16)
-                rest = (part - high.astype(F32)).astype(BF16)
-                span = slice(tap_col * cols, (tap_col + 1) * cols)
-                high_ref[16 * row : 16 * row + 16, span] = high
-                rest_ref[16 * row : 16 * row + 16, span] = rest
+            taps = dot(win_ref[...], target[...], 1, 1)
+            upper = taps.astype(BF16)
+            lower = (taps - upper.astype(F32)).astype(BF16)
+            for row in range(low, high):
+                place = slice((row - low) * cols, (row - low + 1) * cols)
+                for tap_col in range(3):
+                    taken = slice(16 * tap_col, 16 * tap_col + 16)
+                    span = slice(tap_col * cols, (tap_col + 1) * cols)
+                    high_ref[16 * row : 16 * row + 16, span] = upper[taken, place]
+                    rest_ref[16 * row : 16 * row + 16, span] = lower[taken, place]
 
         return run
 
     lane_parts = [spans(low) for low in range(0, chans, LANES)]
     queue = []
-    for row in range(hidden_rows):
-        queue += [(("hidden", row), -1, hidden_piece(row, lanes)) for lanes in lane_parts]
+    done, each = 0, CHUNK * tiles // cols
+    for number, (_, high) in enumerate(mixed_chunks):
+        buf, reach = m_refs[(number + 1) % len(m_refs)], min(high + 2, hidden_rows)
+        groups = [range(low, min(low + each, reach)) for low in range(done, reach, each)]
+        for plane, group in enumerate(groups):
+            queue.append((("hidden", group[0]), -1, hidden_matmul(buf, plane, group)))
+        for plane, group in enumerate(groups):
+            for spot, row in enumerate(group):
+                queue += [
+                    (("hidden", row), -1, hidden_piece(buf, plane, spot, row, lanes))
+                    for lanes in lane_parts
+                ]
+        done = reach
     for number, (low, high) in enumerate(mixed_chunks):
         buf = m_refs[number % len(m_refs)]
         for row in range(low, high):
@@ -362,7 +385,7 @@
                 (("grad", row), number, grad_piece(buf, row, low, target, lanes))
                 for lanes in lane_parts
             ]
-            queue.append((("back", row), number, back_piece(row, low, target)))
+        queue.append((("back", low), number, back_piece(low, high, target)))
     queue.reverse()
 
     def flush(needed):

time: 65.1 us -> 64.5 us (level)
  Pallas kernels: 44.9 us -> 44.2 us
  transfers between devices with their start and end apart: 6 -> 6, of which waited for: 3 -> 3; matrix products, arithmetic and copies ran while one was open for 0% -> 0% of each run, Pallas kernels for 10% -> 11%
where the time goes in v2:
time: 64.5 us; the launch traced here: 64.3 us
  Pallas kernels  44.2 us (69%)
  starting transfers between devices  9.45 us (15%)
  blocking collectives  5.64 us (9%)
  waiting for transfers between devices  2.7 us (4%)
  between operations  1.6 us (2%)
    pallas_call x4, Pallas kernels, call(): pl.pallas_call(kernel, in_specs=[SMEM] * len(scalars) + [VMEM] * len(oper...  40.9 us
    ppermute x3, starting transfers between devices, body(): lax.ppermute(weight_grad, 'dp', [(i, i ^ stage) for i in range(images)])  6.27 us
    all_gather x1, blocking collectives, body(): full = lax.all_gather(noise, 'mp', axis=0, tiled=True)  5.64 us
    pallas_call x2, Pallas kernels, feature_call(): pl.pallas_call(functools.partial(feature_kernel, first=first, lat=lat), g...  3.31 us
    ppermute x3, starting transfers between devices, body(): lax.ppermute(blocks[part], 'mp', [(i, i ^ part) for i in range(parts)])  3.18 us
    ppermute x3, waiting for transfers between devices, body(): lax.ppermute(weight_grad, 'dp', [(i, i ^ stage) for i in range(images)])  2.69 us
  transfers between devices with their start and end apart: 6, of which 3 were waited for; matrix products, arithmetic and copies ran while one was open for 0% of the time, Pallas kernels for 11%

profile of v2, /device:TPU:0, one launch (start us, length us, event | category | flops | bytes accessed | tf_op | source)
XLA Modules:
  0.0 64.3 jit_solution(11247114272203190459)
XLA Ops:
  0.6 0.0 copy-start.7
  0.6 0.0 copy-start.3
  0.7 0.0 copy-start.4
  0.7 0.0 copy-start.10
  0.7 0.0 copy-start.9
  1.5 3.9 %eps_partial.1 = (bf16[160,128]{1,0:T(8,128)(2,1)S(1)}, bf16[160,128]{1,0:T(8,128)(2,1)S(1)}, bf16[160,128]{1,0:T(8,128)(2,1)S(1)}, bf16[160,128]{1,0:T(8,128)(2,1)S(1)}, bf16[216,1280]{1,0:T(8,128)(2,1)S(1)}) custom-call(s32[1]{0:T(128)S(6)} %copy.21.step_ref, s32[1]{0:T(128)} %bitcast.me_ref, bf16[36,80]{1,0:T(8,128)(2,1)} %bitcast.17, ...), custom_call_target="tpu_custom_call" | custom-call | tf_op jit(solution)/shard_map/eps_partial/pallas_call | solution.py:531
  5.3 0.5 collective-permute-start
  5.9 2.6 %collective-permute-start.1 = (bf16[160,128]{1,0:T(8,128)(2,1)S(1)}, bf16[160,128]{1,0:T(8,128)(2,1)S(1)}, u32[]{:S(2)}, u32[]{:S(2)}) collective-permute-start(bf16[160,128]{1,0:T(8,128)(2,1)S(1)} %get-tuple-element.16), channel_id=1, source_target_pairs={{0,2},{1,3},{2,0},{3,1},{4,6},{5,7},{6,4},{7,5},{8,10},{9,11},{10,... | collective-permute-start | bytes 122888 | tf_op jit(solution)/shard_map/ppermute | solution.py:663
  8.5 0.1 collective-permute-start.2
  8.5 3.5 %weight_planes.1 = (bf16[4,3,512,512]{3,2,1,0:T(8,128)(2,1)S(1)}, bf16[9,512,512]{2,1,0:T(8,128)(2,1)S(1)}, bf16[1280,216]{1,0:T(8,128)(2,1)S(1)}) custom-call(bf16[216,1280]{1,0:T(8,128)(2,1)S(1)} %get-tuple-element.12.band_ref, bf16[9,512,512]{2,1,0:T(8,128)(2,1)} %wmid_hbm.1), custom_call_target="tpu_custom_call" | custom-call | tf_op jit(solution)/shard_map/weight_planes/pallas_call | solution.py:531
  12.0 0.0 collective-permute-done.refs_1_
  12.0 0.0 collective-permute-done.1.refs_2_
  12.0 0.0 collective-permute-done.2.refs_3_
  12.1 0.0 copy-start
  12.1 0.0 copy-start.1
  12.1 0.0 copy-start.2
  12.2 0.0 copy-start.5
  12.2 0.0 copy-start.11
  12.2 32.1 %decoder.1 = bf16[128,128]{1,0:T(8,128)(2,1)} custom-call(s32[1]{0:T(128)S(6)} %copy.21.step_ref, s32[1]{0:T(128)} %bitcast.me_ref, bf16[160,128]{1,0:T(8,128)(2,1)S(1)} %get-tuple-element.14.refs_0_, bf16[160,128]{1,0:T(8,128)(2,1)S(1)} %collective-permute-done.refs_1_, bf16[160,128]{1,0:T(8,128)(2,1)S(1)} %collective-permute-done.1.refs_2_, ...), custom_call_target="tpu_custom_call" | custom-call | tf_op jit(solution)/shard_map/decoder/pallas_call | solution.py:531
  44.2 5.6 %all_gather.3.noise_ref = bf16[512,128]{1,0:T(8,128)(2,1)S(1)} all-gather(bf16[128,128]{1,0:T(8,128)(2,1)} %decoder.1), channel_id=1, replica_groups=mesh['dp'=8,'mp'=4] {'mp'}, dimensions={0}, use_global_device_ids=true | all-gather | bytes 163840 | tf_op jit(solution)/shard_map/all_gather | solution.py:671
  49.9 0.0 copy-done.5
  49.9 0.0 copy-done.11
  49.9 1.5 %weight_grad.1 = f32[36,80]{1,0:T(8,128)S(1)} custom-call(bf16[512,128]{1,0:T(8,128)(2,1)S(1)} %all_gather.3.noise_ref, bf16[240,1280]{1,0:T(8,128)(2,1)S(1)} %copy-done.2, bf16[3,36,216]{2,1,0:T(8,128)(2,1)S(1)} %copy-done.5, s32[1,216]{1,0:T(1,128)S(1)} %copy-done.11, s32[1280,1]{1,0:T(8,128)S(1)} %copy-done.1, bf16[80,128,128]{2,1,0:T(8,128)(2,1)S(1)} %bitcast.11), custom_call_target="tpu_custom_call" | custom-call | tf_op jit(solution)/shard_map/weight_grad/pallas_call | solution.py:531
  51.4 1.7 %collective-permute-start.3 = (f32[36,80]{1,0:T(8,128)S(1)}, f32[36,80]{1,0:T(8,128)S(1)}, u32[]{:S(2)}, u32[]{:S(2)}) collective-permute-start(f32[36,80]{1,0:T(8,128)S(1)} %weight_grad.1), channel_id=1, source_target_pairs={{0,4},{4,0},{8,12},{12,8},{16,20},{20,16},{24,28},{28,24},{1,5},{5... | collective-permute-start | bytes 34568 | tf_op jit(solution)/shard_map/ppermute | solution.py:676
  53.1 1.7 %feature_grads.2.refs_0_ = bf16[80,128,128]{2,1,0:T(8,128)(2,1)} custom-call(bf16[1280,216]{1,0:T(8,128)(2,1)S(1)} %get-tuple-element.13.band_ref, bf16[512,128]{1,0:T(8,128)(2,1)S(1)} %all_gather.3.noise_ref), custom_call_target="tpu_custom_call" | custom-call | tf_op jit(solution)/shard_map/feature_grads/pallas_call | solution.py:631
  54.8 0.4 collective-permute-done.3
  55.2 1.8 %collective-permute-start.4 = (f32[36,80]{1,0:T(8,128)S(1)}, f32[36,80]{1,0:T(8,128)S(1)}, u32[]{:S(2)}, u32[]{:S(2)}) collective-permute-start(f32[36,80]{1,0:T(8,128)S(1)} %add.9), channel_id=1, source_target_pairs={{0,8},{4,12},{8,0},{12,4},{16,24},{20,28},{24,16},{28,20},{1,9},{5... | collective-permute-start | bytes 34568 | tf_op jit(solution)/shard_map/ppermute | solution.py:676
  57.0 2.0 %collective-permute-done.4 = f32[36,80]{1,0:T(8,128)S(1)} collective-permute-done((f32[36,80]{1,0:T(8,128)S(1)}, f32[36,80]{1,0:T(8,128)S(1)}, u32[]{:S(2)}, u32[]{:S(2)}) %collective-permute-start.4) | collective-permute-done | bytes 11552 | tf_op jit(solution)/shard_map/ppermute | solution.py:676
  59.0 2.8 %collective-permute-start.5 = (f32[36,80]{1,0:T(8,128)S(1)}, f32[36,80]{1,0:T(8,128)S(1)}, u32[]{:S(2)}, u32[]{:S(2)}) collective-permute-start(f32[36,80]{1,0:T(8,128)S(1)} %add.10), channel_id=1, source_target_pairs={{0,16},{4,20},{8,24},{12,28},{16,0},{20,4},{24,8},{28,12},{1,17},{... | collective-permute-start | bytes 34568 | tf_op jit(solution)/shard_map/ppermute | solution.py:676
  61.8 1.7 %feature_grads.3 = bf16[80,128,128]{2,1,0:T(8,128)(2,1)} custom-call(bf16[1280,216]{1,0:T(8,128)(2,1)S(1)} %get-tuple-element.13.band_ref, bf16[512,128]{1,0:T(8,128)(2,1)S(1)} %all_gather.3.noise_ref, bf16[80,128,128]{2,1,0:T(8,128)(2,1)} %feature_grads.2.refs_0_), custom_call_target="tpu_custom_call", output_to_operand_aliasing={{}: (2, {})} | custom-call | tf_op jit(solution)/shard_map/feature_grads/pallas_call | solution.py:631
  63.4 0.2 collective-permute-done.5
  63.7 0.6 multiply_bitcast_fusion
  (14 shorter events, 0.0 us)
Async XLA Ops:
  0.6 11.4 %copy-start.7 = (f32[8,128]{1,0:T(8,128)S(1)}, f32[8,128]{1,0:T(8,128)}, u32[]{:S(2)}) copy-start(f32[8,128]{1,0:T(8,128)} %constant.23.clone.table_ref.refs_4_) | copy-start | bytes 12292
  0.6 11.4 %copy-start.3 = (bf16[384,128]{1,0:T(8,128)(2,1)S(1)}, bf16[384,128]{1,0:T(8,128)(2,1)}, u32[]{:S(2)}) copy-start(bf16[384,128]{1,0:T(8,128)(2,1)} %constant.25.clone.refs_6_) | copy-start | bytes 294916
  0.7 11.4 %copy-start.4 = (bf16[3,128,128]{2,1,0:T(8,128)(2,1)S(1)}, bf16[3,128,128]{2,1,0:T(8,128)(2,1)}, u32[]{:S(2)}) copy-start(bf16[3,128,128]{2,1,0:T(8,128)(2,1)} %constant.24.clone.refs_5_) | copy-start | bytes 294916
  0.7 11.4 %copy-start.10 = (f32[512]{0:T(512)S(1)}, f32[512]{0:T(512)}, u32[]{:S(2)}) copy-start(f32[512]{0:T(512)} %param.25) | copy-start | bytes 6148
  0.7 11.4 %copy-start.9 = (f32[512]{0:T(512)S(1)}, f32[512]{0:T(512)}, u32[]{:S(2)}) copy-start(f32[512]{0:T(512)} %param.24) | copy-start | bytes 6148
  0.7 11.4 %copy-start.8 = (f32[512]{0:T(512)S(1)}, f32[512]{0:T(512)}, u32[]{:S(2)}) copy-start(f32[512]{0:T(512)} %param.22) | copy-start | bytes 6148
  0.7 11.4 %copy-start.6 = (bf16[9,512,4]{1,2,0:T(4,128)(2,1)S(1)}, bf16[9,512,4]{1,2,0:T(4,128)(2,1)}, u32[]{:S(2)}) copy-start(bf16[9,512,4]{1,2,0:T(4,128)(2,1)} %param.21) | copy-start | bytes 110596
  5.3 6.7 %collective-permute-start = (bf16[160,128]{1,0:T(8,128)(2,1)S(1)}, bf16[160,128]{1,0:T(8,128)(2,1)S(1)}, u32[]{:S(2)}, u32[]{:S(2)}) collective-permute-start(bf16[160,128]{1,0:T(8,128)(2,1)S(1)} %get-tuple-element.15), channel_id=1, source_target_pairs={{0,1},{1,0},{2,3},{3,2},{4,5},{5,4},{6,7},{7,6},{8,9},{9,8},{10,11... | collective-permute-start | bytes 122888 | tf_op jit(solution)/shard_map/ppermute | solution.py:663
  5.9 6.2 %collective-permute-start.1 = (bf16[160,128]{1,0:T(8,128)(2,1)S(1)}, bf16[160,128]{1,0:T(8,128)(2,1)S(1)}, u32[]{:S(2)}, u32[]{:S(2)}) collective-permute-start(bf16[160,128]{1,0:T(8,128)(2,1)S(1)} %get-tuple-element.16), channel_id=1, source_target_pairs={{0,2},{1,3},{2,0},{3,1},{4,6},{5,7},{6,4},{7,5},{8,10},{9,11},{10,... | collective-permute-start | bytes 122888 | tf_op jit(solution)/shard_map/ppermute | solution.py:663
  8.5 3.6 %collective-permute-start.2 = (bf16[160,128]{1,0:T(8,128)(2,1)S(1)}, bf16[160,128]{1,0:T(8,128)(2,1)S(1)}, u32[]{:S(2)}, u32[]{:S(2)}) collective-permute-start(bf16[160,128]{1,0:T(8,128)(2,1)S(1)} %get-tuple-element.17), channel_id=1, source_target_pairs={{0,3},{1,2},{2,1},{3,0},{4,7},{5,6},{6,5},{7,4},{8,11},{9,10},{10,... | collective-permute-start | bytes 122888 | tf_op jit(solution)/shard_map/ppermute | solution.py:663
  12.1 37.8 %copy-start = (bf16[1,80,128,128]{3,2,1,0:T(8,128)(2,1)S(1)}, bf16[1,80,128,128]{3,2,1,0:T(8,128)(2,1)}, u32[]{:S(2)}) copy-start(bf16[1,80,128,128]{3,2,1,0:T(8,128)(2,1)} %param.17) | copy-start | bytes 7864324
  12.1 37.8 %copy-start.1 = (s32[1280,1]{1,0:T(8,128)S(1)}, s32[1280,1]{1,0:T(8,128)}, u32[]{:S(2)}) copy-start(s32[1280,1]{1,0:T(8,128)} %constant.27.clone.in_row_ref) | copy-start | bytes 15364
  12.1 37.7 %copy-start.2 = (bf16[240,1280]{1,0:T(8,128)(2,1)S(1)}, bf16[240,1280]{1,0:T(8,128)(2,1)}, u32[]{:S(2)}) copy-start(bf16[240,1280]{1,0:T(8,128)(2,1)} %constant.21.clone.thirds_ref) | copy-start | bytes 1843204
  12.2 37.7 %copy-start.5 = (bf16[3,36,216]{2,1,0:T(8,128)(2,1)S(1)}, bf16[3,36,216]{2,1,0:T(8,128)(2,1)}, u32[]{:S(2)}) copy-start(bf16[3,36,216]{2,1,0:T(8,128)(2,1)} %constant.22.clone.collect_ref) | copy-start | bytes 139972
  12.2 37.7 %copy-start.11 = (s32[1,216]{1,0:T(1,128)S(1)}, s32[1,216]{1,0:T(1,128)}, u32[]{:S(2)}) copy-start(s32[1,216]{1,0:T(1,128)} %constant.26.clone.out_row_ref) | copy-start | bytes 2596
  51.4 3.8 %collective-permute-start.3 = (f32[36,80]{1,0:T(8,128)S(1)}, f32[36,80]{1,0:T(8,128)S(1)}, u32[]{:S(2)}, u32[]{:S(2)}) collective-permute-start(f32[36,80]{1,0:T(8,128)S(1)} %weight_grad.1), channel_id=1, source_target_pairs={{0,4},{4,0},{8,12},{12,8},{16,20},{20,16},{24,28},{28,24},{1,5},{5... | collective-permute-start | bytes 34568 | tf_op jit(solution)/shard_map/ppermute | solution.py:676
  55.2 3.8 %collective-permute-start.4 = (f32[36,80]{1,0:T(8,128)S(1)}, f32[36,80]{1,0:T(8,128)S(1)}, u32[]{:S(2)}, u32[]{:S(2)}) collective-permute-start(f32[36,80]{1,0:T(8,128)S(1)} %add.9), channel_id=1, source_target_pairs={{0,8},{4,12},{8,0},{12,4},{16,24},{20,28},{24,16},{28,20},{1,9},{5... | collective-permute-start | bytes 34568 | tf_op jit(solution)/shard_map/ppermute | solution.py:676
  59.0 4.7 %collective-permute-start.5 = (f32[36,80]{1,0:T(8,128)S(1)}, f32[36,80]{1,0:T(8,128)S(1)}, u32[]{:S(2)}, u32[]{:S(2)}) collective-permute-start(f32[36,80]{1,0:T(8,128)S(1)} %add.10), channel_id=1, source_target_pairs={{0,16},{4,20},{8,24},{12,28},{16,0},{20,4},{24,8},{28,12},{1,17},{... | collective-permute-start | bytes 34568 | tf_op jit(solution)/shard_map/ppermute | solution.py:676
